TPU v7x, 32 devices: a whole 2x2x4 slice. The times are simulated.
32 devices in a mesh: ctx: 8 (over z, y), tp: 4 (over x, core).
Axes of the slice: x: 2, y: 2, z: 4, core: 2. Of those that a mesh axis runs over, the one named last changes fastest.
Arguments:
- queries: bfloat16 [1024, 5120], P('ctx', 'tp'), may hold values from -40 to 40
- keys: bfloat16 [1024, 1024], P('ctx', 'tp'), may hold values from -40 to 40
- values: bfloat16 [1024, 1024], P('ctx', 'tp'), may hold values from -6 to 6
- out_grad: bfloat16 [1024, 5120], P('ctx', 'tp'), may hold values from -6 to 6
- ancestry: int32 [8, 5], replicated, may hold values from 0 to 7, as said below
- w_query: bfloat16 [5120, 5120], P(None, 'tp'), may hold values from -0.078125 to 0.078125
- key_matrix: bfloat16 [5120, 1024], P(None, 'tp'), may hold values from -0.078125 to 0.078125
- value_matrix: bfloat16 [5120, 1024], P(None, 'tp'), may hold values from -0.078125 to 0.078125
Outputs:
- input_grad: bfloat16 [1024, 5120], P('ctx', 'tp')
Inputs may be any that keep to these rules, and one draw needn't show every extreme that they name: `ancestry`: row b holds b, then its ancestors in order parent, grandparent and so on (each an earlier block), then b again to fill the row. Blocks 0 to 4 form one chain, each the parent of the next; no block has more than 4 ancestors; every block descends from blocks 0 to 0 or is one of them.
All inputs are finite; a program needn't handle non-finite values.
Results may differ from a plain program's by a relative error of at most 0.024.
Values may be sent and summed in bfloat16 or wider, within the bound.
A program may use at most 128 MiB of HBM per device.

v0:
```python
import math

import jax
import jax.numpy as jnp
from jax import lax
from jax.sharding import PartitionSpec as P

HEAD_SIZE = 128
TREE_BLOCK_SIZE = 128


ROPE_BASE = 1000000.0
MASKED = -1e30


def inverse_rotary(grads, token_places):
    half_width = grads.shape[-1] // 2
    frequencies = jnp.exp(
        jnp.arange(half_width, dtype=jnp.float32) * (-2.0 * math.log(ROPE_BASE) / grads.shape[-1])
    )
    angles = token_places[:, None] * frequencies[None, :]
    cosine = jnp.cos(angles)[:, None, :]
    sine_part = jnp.sin(angles)[:, None, :]
    front_half = grads[..., :half_width]
    second = grads[..., half_width:]
    return jnp.concatenate(
        [front_half * cosine + second * sine_part, second * cosine - front_half * sine_part],
        axis=-1,
    )


def to_rows(matrix, kv_local):
    row_count = matrix.shape[0]
    heads_per_group = matrix.shape[1] // HEAD_SIZE // kv_local
    return (
        matrix.reshape(row_count, kv_local, heads_per_group, HEAD_SIZE)
        .transpose(1, 2, 0, 3)
        .reshape(kv_local, heads_per_group * row_count, HEAD_SIZE)
    )


def spread_mask(seen_mask, kv_local, heads_per_group):
    reshaped_tensor = jnp.broadcast_to(
        seen_mask[None, None], (kv_local, heads_per_group) + seen_mask.shape
    )
    return reshaped_tensor.reshape(
        kv_local, heads_per_group * seen_mask.shape[0], seen_mask.shape[1]
    )


def visible_mask(ancestry, query_tok, key_tok):
    query_blk = query_tok // TREE_BLOCK_SIZE
    key_blk = key_tok // TREE_BLOCK_SIZE
    every_block = jnp.arange(ancestry.shape[0], dtype=jnp.int32)
    listed = jnp.any(ancestry[:, :, None] == key_blk[None, None, :], axis=1).astype(jnp.float32)
    picker = (query_blk[:, None] == every_block[None, :]).astype(jnp.float32)
    hit_rows = jnp.dot(picker, listed) > 0.5
    causal = (query_blk[:, None] != key_blk[None, :]) | (key_tok[None, :] <= query_tok[:, None])
    return hit_rows & causal


def local_fold(step_fn, initial, keys_all, values_all):
    all_tokens = keys_all.shape[0]
    span_rows = min(all_tokens, 4 * TREE_BLOCK_SIZE)

    def turn(turn_id, current):
        offset = turn_id * span_rows
        portion = (
            lax.dynamic_slice_in_dim(keys_all, offset, span_rows, 0),
            lax.dynamic_slice_in_dim(values_all, offset, span_rows, 0),
        )
        return step_fn(current, portion, offset)

    return lax.fori_loop(0, all_tokens // span_rows, turn, initial)


def shards(queries, keys, values, out_grad, ancestry, w_query, key_matrix, value_matrix):
    tok_local = queries.shape[0]
    kv_local = keys.shape[1] // HEAD_SIZE
    heads_local = queries.shape[1] // HEAD_SIZE
    heads_per_group = heads_local // kv_local
    factor = HEAD_SIZE ** (-0.5)
    all_tokens = tok_local * lax.axis_size("ctx")
    my_start = lax.axis_index("ctx") * tok_local
    own_tok = my_start + jnp.arange(tok_local, dtype=jnp.int32)
    every_block = jnp.arange(ancestry.shape[0], dtype=jnp.int32)
    depths = jnp.sum((ancestry != every_block[:, None]).astype(jnp.int32), axis=1)
    own_block = own_tok // TREE_BLOCK_SIZE
    own_depth = jnp.sum(
        jnp.where(own_block[:, None] == every_block[None, :], depths[None, :], 0), axis=1
    )
    token_places = (TREE_BLOCK_SIZE * own_depth + own_tok % TREE_BLOCK_SIZE).astype(jnp.float32)
    query_rows = to_rows(queries, kv_local)
    grad_rows = to_rows(out_grad, kv_local)
    row_count = heads_per_group * tok_local

    def forward_step(carry_state, portion, offset):
        keys_part, values_part = portion
        count_rows = keys_part.shape[0]
        key_tok = offset + jnp.arange(count_rows, dtype=jnp.int32)
        seen_mask = visible_mask(ancestry, own_tok, key_tok)

        def forward_update(current):
            maxima, totals, running = current
            heads_of_key = keys_part.reshape(count_rows, kv_local, HEAD_SIZE)
            heads_of_value = values_part.reshape(count_rows, kv_local, HEAD_SIZE)
            seen_rows = spread_mask(seen_mask, kv_local, heads_per_group)
            scores = (
                jnp.einsum(
                    "hrd,nhd->hrn", query_rows, heads_of_key, preferred_element_type=jnp.float32
                )
                * factor
            )
            scores = jnp.where(seen_rows, scores, MASKED)
            highest = jnp.maximum(maxima, jnp.max(scores, axis=-1))
            weights = jnp.where(seen_rows, jnp.exp(scores - highest[:, :, None]), 0.0)
            shrink = jnp.exp(maxima - highest)
            totals = totals * shrink + jnp.sum(weights, axis=-1)
            running = running * shrink[:, :, None] + jnp.einsum(
                "hrn,nhd->hrd",
                weights.astype(jnp.bfloat16),
                heads_of_value,
                preferred_element_type=jnp.float32,
            )
            return (highest, totals, running)

        return lax.cond(jnp.any(seen_mask), forward_update, lambda current: current, carry_state)

    start_state = (
        jnp.full((kv_local, row_count), MASKED, jnp.float32),
        jnp.zeros((kv_local, row_count), jnp.float32),
        jnp.zeros((kv_local, row_count, HEAD_SIZE), jnp.float32),
    )
    keys_all, values_all = (
        lax.all_gather(keys, "ctx", axis=0, tiled=True),
        lax.all_gather(values, "ctx", axis=0, tiled=True),
    )
    maxima, totals, running = local_fold(forward_step, start_state, keys_all, values_all)
    attended = (running / totals[:, :, None]).astype(jnp.bfloat16)
    log_totals = maxima + jnp.log(totals)
    row_dots = jnp.sum(grad_rows.astype(jnp.float32) * attended.astype(jnp.float32), axis=-1)
    pair_width = 2 * kv_local * HEAD_SIZE

    def backward_step(carry_state, portion, offset):
        keys_part, values_part = portion
        count_rows = keys_part.shape[0]
        key_tok = offset + jnp.arange(count_rows, dtype=jnp.int32)
        seen_mask = visible_mask(ancestry, own_tok, key_tok)

        def backward_update(current):
            heads_of_key = keys_part.reshape(count_rows, kv_local, HEAD_SIZE)
            heads_of_value = values_part.reshape(count_rows, kv_local, HEAD_SIZE)
            seen_rows = spread_mask(seen_mask, kv_local, heads_per_group)
            scores = (
                jnp.einsum(
                    "hrd,nhd->hrn", query_rows, heads_of_key, preferred_element_type=jnp.float32
                )
                * factor
            )
            weights = jnp.where(seen_rows, jnp.exp(scores - log_totals[:, :, None]), 0.0)
            prob_grads = jnp.einsum(
                "hrd,nhd->hrn", grad_rows, heads_of_value, preferred_element_type=jnp.float32
            )
            score_grads = (weights * (prob_grads - row_dots[:, :, None])).astype(jnp.bfloat16)
            query_grad = (
                current[0]
                + jnp.einsum(
                    "hrn,nhd->hrd", score_grads, heads_of_key, preferred_element_type=jnp.float32
                )
                * factor
            )
            key_grad = (
                jnp.einsum(
                    "hrn,hrd->nhd", score_grads, query_rows, preferred_element_type=jnp.float32
                )
                * factor
            )
            value_grad = jnp.einsum(
                "hrn,hrd->nhd",
                weights.astype(jnp.bfloat16),
                grad_rows,
                preferred_element_type=jnp.float32,
            )
            stacked = jnp.concatenate(
                [
                    key_grad.reshape(count_rows, kv_local * HEAD_SIZE),
                    value_grad.reshape(count_rows, kv_local * HEAD_SIZE),
                ],
                axis=1,
            )
            return (query_grad, lax.dynamic_update_slice_in_dim(current[1], stacked, offset, 0))

        return lax.cond(jnp.any(seen_mask), backward_update, lambda current: current, carry_state)

    back_state = (jnp.zeros((kv_local, row_count, HEAD_SIZE), jnp.float32),) + (
        jnp.zeros((all_tokens, pair_width), jnp.float32),
    )
    finished = local_fold(backward_step, back_state, keys_all, values_all)
    summed = lax.psum_scatter(
        finished[1].astype(jnp.bfloat16), "ctx", scatter_dimension=0, tiled=True
    ).astype(jnp.float32)
    key_own = summed[:, : kv_local * HEAD_SIZE].reshape(tok_local, kv_local, HEAD_SIZE)
    value_own = summed[:, kv_local * HEAD_SIZE :]
    query_total = (
        finished[0]
        .reshape(kv_local, heads_per_group, tok_local, HEAD_SIZE)
        .transpose(2, 0, 1, 3)
        .reshape(tok_local, heads_local, HEAD_SIZE)
    )
    query_low = (
        inverse_rotary(query_total, token_places)
        .astype(jnp.bfloat16)
        .reshape(tok_local, heads_local * HEAD_SIZE)
    )
    key_reduced = (
        inverse_rotary(key_own, token_places)
        .astype(jnp.bfloat16)
        .reshape(tok_local, kv_local * HEAD_SIZE)
    )
    value_reduced = value_own.astype(jnp.bfloat16)
    contract = (((1,), (1,)), ((), ()))
    partial_sum = lax.dot_general(query_low, w_query, contract, preferred_element_type=jnp.float32)
    partial_sum = partial_sum + lax.dot_general(
        key_reduced, key_matrix, contract, preferred_element_type=jnp.float32
    )
    partial_sum = partial_sum + lax.dot_general(
        value_reduced, value_matrix, contract, preferred_element_type=jnp.float32
    )
    return lax.psum_scatter(partial_sum.astype(jnp.bfloat16), "tp", scatter_dimension=1, tiled=True)


def solution(mesh):
    in_specs = (
        P("ctx", "tp"),
        P("ctx", "tp"),
        P("ctx", "tp"),
        P("ctx", "tp"),
        P(),
        P(None, "tp"),
        P(None, "tp"),
        P(None, "tp"),
    )
    out_specs = P("ctx", "tp")
    return jax.shard_map(shards, mesh=mesh, in_specs=in_specs, out_specs=out_specs, check_vma=False)
```

profile of v0, /device:TPU:0, one launch (start us, length us, event | category | flops | bytes accessed | tf_op | source)
XLA Modules:
  0.0 237.1 jit_solution(2011096044275631273)
XLA Ops:
  6.5 1.3 copy.81
  7.9 0.9 copy.82
  8.8 0.9 copy.80
  9.8 30.8 %all_gather.6 = bf16[1024,256]{0,1:T(8,128)(2,1)} all-gather(bf16[128,256]{0,1:T(8,128)(2,1)S(1)} %copy.80), channel_id=1, replica_groups=mesh['ctx'=8,'tp'=4] {'ctx'}, dimensions={0}, use_global_device_ids=true | all-gather | bytes 589824 | tf_op jit(solution)/shard_map/all_gather | solution.py:135
  40.5 0.9 copy.83
  41.5 28.6 %all_gather.7 = bf16[1024,256]{0,1:T(8,128)(2,1)} all-gather(bf16[128,256]{0,1:T(8,128)(2,1)S(1)} %copy.83), channel_id=1, replica_groups=mesh['ctx'=8,'tp'=4] {'ctx'}, dimensions={0}, use_global_device_ids=true | all-gather | bytes 589824 | tf_op jit(solution)/shard_map/all_gather | solution.py:136
  70.2 1.2 copy.88
  71.4 0.9 broadcast.658.clone
  72.3 0.6 broadcast_in_dim.123
  72.9 13.5 %while.42 = (s32[]{:T(128)}, f32[2,640]{1,0:T(2,128)S(1)}, f32[2,640]{1,0:T(2,128)}, f32[2,640,128]{2,1,0:T(8,128)}, s32[8,5]{0,1:T(8,128)S(1)}, /*index=5*/bf16...) while((s32[]{:T(128)}, f32[2,640]{1,0:T(2,128)S(1)}, ...), condition=%wide.region_7.8_spmd.clone.clone, body=%wide.region_0.7_spmd.clone.clone.sunk | while | flops 345884288 | bytes 19567128 | solution.py:74
  73.0 0.9 fusion.82
  74.5 10.1 %conditional.8 = ((f32[2,640]{1,0:T(2,128)S(1)}, f32[2,640]{1,0:T(2,128)}, f32[2,640,128]{2,1,0:T(8,128)})) conditional(s32[]{:T(128)} %convert_element_type.119, (f32[2,640]{1,0:T(2,128)S(1)}, f32[2,640]{1,0:T(2,128)}, f32[2,640,128]{2,1,0:T(8,128)}) %tuple.159, (pred[128,512]{1,0:T(8,128)(4,1)S(1)}, s32[]{:T(128)}, bf16[1024,256]{0,1:T(8,128)(2,1)}, ...), branch_computations={%region_3.3_spmd, %region_4.6_spmd} | conditional | flops 344394240 | bytes 19480730 | solution.py:127
  74.6 1.8 constant_dynamic-slice_fusion
  76.3 0.8 broadcast_in_dim.107
  77.2 1.5 copy.67
  78.6 1.8 fusion.12
  80.5 0.7 fusion.14
  81.2 1.3 multiply_add_fusion
  82.5 1.3 fusion.18
  83.8 0.8 copy-done.10
  84.7 0.9 fusion.82
  86.3 1.9 copy.85
  88.2 1.2 copy.86
  89.4 1.3 log_add_fusion
  90.7 2.1 multiply_reduce_fusion
  92.8 0.9 copy.89
  93.7 1.1 broadcast_in_dim.121
  94.8 0.9 broadcast.658
  95.7 16.6 %while.43 = (s32[]{:T(128)}, f32[2,640,128]{2,1,0:T(8,128)}, bf16[1024,512]{0,1:T(8,128)(2,1)}, s32[8,5]{0,1:T(8,128)S(1)}, bf16[1024,256]{0,1:T(8,128)(2,1)}, /...) while((s32[]{:T(128)}, f32[2,640,128]{2,1,0:T(8,128)}, ...), condition=%wide.region_14.15_spmd.clone.clone, body=%wide.region_9.14_spmd.clone.clone.sunk | while | flops 848542848 | bytes 46632632 | solution.py:74
  95.9 1.5 fusion.85
  98.0 12.0 %conditional.9 = ((f32[2,640,128]{2,1,0:T(8,128)}, bf16[1024,512]{0,1:T(8,128)(2,1)})) conditional(s32[]{:T(128)} %convert_element_type.120, (f32[2,640,128]{2,1,0:T(8,128)}, bf16[1024,512]{0,1:T(8,128)(2,1)}) %tuple.165, (pred[128,512]{1,0:T(8,128)(4,1)}, s32[]{:T(128)}, bf16[1024,256]{0,1:T(8,128)(2,1)}, bf16[2,640,128]{1,2,0:T(8,128)(2,1)S(1)}, ...), branch_computations={%region_12.12_spmd, %region_13.13_spmd} | conditional | flops 847052800 | bytes 46546212 | solution.py:193
  98.1 1.8 constant_dynamic-slice_fusion.2
  99.9 2.1 fusion.53
  102.0 1.2 copy.71
  103.2 3.1 %fusion.24 = bf16[2,640,512]{1,2,0:T(8,128)(2,1)S(1)} fusion(f32[2,512,640]{2,1,0:T(8,128)} %fusion.53, bf16[512,2,128]{0,2,1:T(8,128)(2,1)} %bitcast.109, bf16[2,640,128]{1,2,0:T(8,128)(2,1)} %get-tuple-element.819, f32[2,640]{1,0:T(2,128)} %get-tuple-element.820, f32[2,640]{1,0:T(2,128)S(1)} %get-tuple-element.817, pred[640,512]{0,1:T(8,128)(4,1)} %copy.71), kind=kOutput, calls=%fused_computation.22 | convolution fusion | flops 171704320 | bytes 4859904 | tf_op jit(solution)/shard_map/while/body/eval_jaxpr/cond/branch_1_fun/hrd,nhd->hrn/dot_general | solution.py:161
  106.9 0.9 fusion.26
  108.3 0.7 fusion.32
  109.2 0.8 copy-done.3
  110.2 1.5 fusion.85
  112.4 2.3 copy.102
  114.9 2.2 copy.90
  117.5 1.2 add_convert_fusion
  118.7 10.7 %fusion.54 = f32[128,5120]{1,0:T(8,128)} fusion(bf16[128,1280]{0,1:T(8,128)(2,1)S(1)} %bitcast.115, bf16[5120,1280]{1,0:T(8,128)(2,1)} %param.21), kind=kOutput, calls=%fused_computation.111 | convolution fusion | flops 1677721600 | bytes 16056320 | tf_op jit(solution)/shard_map/dot_general | solution.py:222
  129.4 69.1 %reduce-scatter.7.cloned.1.call-done = bf16[128,512]{1,0:T(8,128)(2,1)} async-done(((bf16[1024,512]{1,0:T(8,128)(2,1)}), bf16[128,512]{1,0:T(8,128)(2,1)}) %reduce-scatter.7.cloned.1.call-update) | async-done | bytes 131088
  198.4 0.8 slice.28
  199.5 2.9 %convolution_add_fusion.1 = f32[128,5120]{1,0:T(8,128)S(1)} fusion(f32[128,5120]{1,0:T(8,128)} %fusion.54, bf16[128,256]{0,1:T(8,128)(2,1)S(1)} %bitcast.116, bf16[5120,256]{1,0:T(8,128)(2,1)S(1)} %copy-done), kind=kOutput, calls=%fused_computation.81 | convolution fusion | flops 336199680 | bytes 7929856 | tf_op jit(solution)/shard_map/dot_general | solution.py:223
  202.4 2.1 fusion.47
  204.5 25.7 %reduce-scatter.5.cloned.1.call-done = bf16[128,1280]{1,0:T(8,128)(2,1)} async-done(((bf16[128,5120]{1,0:T(8,128)(2,1)}), bf16[128,1280]{1,0:T(8,128)(2,1)}) %reduce-scatter.5.cloned.1.call-update) | async-done | bytes 327696 | tf_op jit(solution)/shard_map/reduce_scatter | solution.py:229
  (66 shorter events, 2.7 us)
Async XLA Ops:
  6.5 192.9 %copy-start = (bf16[5120,256]{1,0:T(8,128)(2,1)S(1)}, bf16[5120,256]{1,0:T(8,128)(2,1)}, u32[]{:S(2)}) copy-start(bf16[5120,256]{1,0:T(8,128)(2,1)} %param.22) | copy-start | bytes 7864324
  6.5 63.6 %copy-start.14 = (s32[8,5]{1,0:T(8,128)S(1)}, s32[8,5]{1,0:T(8,128)}, u32[]{:S(2)}) copy-start(s32[8,5]{1,0:T(8,128)} %param.20) | copy-start | bytes 484
  6.5 191.9 %reduce-scatter.7.cloned.1.call-start = ((), (), s32[]{:S(2)}) async-start(), calls=%async_computation.3 | async-start | bytes 1179648
  78.6 3.9 %copy-start.5 = (bf16[512,256]{0,1:T(8,128)(2,1)S(1)}, bf16[512,256]{0,1:T(8,128)(2,1)}, u32[]{:S(2)}) copy-start(bf16[512,256]{0,1:T(8,128)(2,1)} %get-tuple-element.1091) | copy-start | bytes 786436 | tf_op jit(solution)/shard_map/while/body/eval_jaxpr/cond
  78.6 3.9 %copy-start.9 = (f32[2,640,128]{2,1,0:T(8,128)S(1)}, f32[2,640,128]{2,1,0:T(8,128)}, u32[]{:S(2)}) copy-start(f32[2,640,128]{2,1,0:T(8,128)} %get-tuple-element.795) | copy-start | bytes 1966084 | tf_op jit(solution)/shard_map/while/body/eval_jaxpr/cond
  83.8 0.8 copy-start.10
  90.7 5.1 %copy-start.15 = (f32[2,640]{1,0:T(2,128)S(1)}, f32[2,640]{1,0:T(2,128)}, u32[]{:S(2)}) copy-start(f32[2,640]{1,0:T(2,128)} %log_add_fusion) | copy-start | bytes 15364
  98.0 3.9 %copy-start.11 = (pred[128,512]{1,0:T(8,128)(4,1)S(1)}, pred[128,512]{1,0:T(8,128)(4,1)}, u32[]{:S(2)}) copy-start(pred[128,512]{1,0:T(8,128)(4,1)} %get-tuple-element.813) | copy-start | bytes 196612 | tf_op jit(solution)/shard_map/while/body/eval_jaxpr/cond
  103.2 3.7 %copy-start.1 = (f32[2,512,640]{2,1,0:T(8,128)S(1)}, f32[2,512,640]{2,1,0:T(8,128)}, u32[]{:S(2)}) copy-start(f32[2,512,640]{2,1,0:T(8,128)} %fusion.53) | copy-start | bytes 7864324 | tf_op jit(solution)/shard_map/while/body/eval_jaxpr/cond
  103.2 3.7 %copy-start.4 = (pred[640,512]{0,1:T(8,128)(4,1)S(1)}, pred[640,512]{0,1:T(8,128)(4,1)}, u32[]{:S(2)}) copy-start(pred[640,512]{0,1:T(8,128)(4,1)} %copy.71) | copy-start | bytes 983044 | tf_op jit(solution)/shard_map/while/body/eval_jaxpr/cond
  103.2 3.7 %copy-start.12 = (bf16[2,640,128]{1,2,0:T(8,128)(2,1)S(1)}, bf16[2,640,128]{1,2,0:T(8,128)(2,1)}, u32[]{:S(2)}) copy-start(bf16[2,640,128]{1,2,0:T(8,128)(2,1)} %get-tuple-element.819) | copy-start | bytes 983044 | tf_op jit(solution)/shard_map/while/body/eval_jaxpr/cond
  106.9 1.2 copy-start.6
  106.9 1.4 copy-start.2
  108.2 1.0 copy-start.7
  109.2 0.8 copy-start.3
  114.7 115.6 %reduce-scatter.5.cloned.1.call-start = ((), (), s32[]{:S(2)}) async-start(), calls=%async_computation.2 | async-start | bytes 1638400 | tf_op jit(solution)/shard_map/reduce_scatter | solution.py:229
  199.5 2.9 %copy-start.8 = (bf16[5120,256]{1,0:T(8,128)(2,1)S(1)}, bf16[5120,256]{1,0:T(8,128)(2,1)}, u32[]{:S(2)}) copy-start(bf16[5120,256]{1,0:T(8,128)(2,1)} %param.23) | copy-start | bytes 7864324
  199.5 2.9 %copy-start.13 = (bf16[128,512]{1,0:T(8,128)(2,1)S(1)}, bf16[128,512]{1,0:T(8,128)(2,1)}, u32[]{:S(2)}) copy-start(bf16[128,512]{1,0:T(8,128)(2,1)} %reduce-scatter.7.cloned.1.call-done) | copy-start | bytes 393220
Sparse Core Ops, SparseCore 0:
  114.8 83.5 reduce-scatter.6
  204.7 25.5 reduce-scatter.4
where the time goes:
time: 238 us; the launch traced here: 237 us
  waiting for transfers between devices  94.8 us (40%)
  blocking collectives  59.4 us (25%)
  matrix products  31.1 us (13%)
  local copies, waits for them, and re-layouts  27.6 us (12%)
  between operations  13.6 us (6%)
  other arithmetic  7.58 us (3%)
  loops' own time  2.8 us (1%)
    unnamed x3, waiting for transfers between devices  69.1 us
    all_gather x1, blocking collectives, shards(): lax.all_gather(keys, 'ctx', axis=0, tiled=True)  30.8 us
    all_gather x1, blocking collectives, shards(): lax.all_gather(values, 'ctx', axis=0, tiled=True)  28.6 us
    reduce_scatter x1, waiting for transfers between devices, shards(): lax.psum_scatter(partial_sum.astype(jnp.bfloat16), 'tp', scatter_dimensio...  25.7 us
    dot_general x1, matrix products, shards(): lax.dot_general(query_low, w_query, contract, preferred_element_type=jnp....  10.7 us
    unnamed x19, local copies, waits for them, and re-layouts  9.69 us
    dot_general x4, matrix products, visible_mask(): hit_rows = jnp.dot(picker, listed) > 0.5  4.97 us
  transfers between devices with their start and end apart: 2, of which 2 were waited for; matrix products, arithmetic and copies ran while one was open for 6% of the time, Pallas kernels for 0%

commit v1 on v0

v1 whole, which is shorter than its diff:
```python
import functools
import math

import jax
import jax.numpy as jnp
from jax import lax
from jax.experimental import pallas as pl
from jax.experimental.pallas import tpu as pltpu
from jax.sharding import PartitionSpec as P

HEAD_SIZE = 128
ROPE_BASE = 1000000.0
MASKED = -1e30
MESH = pl.DeviceIdType.MESH
F32 = jnp.float32
BF16 = jnp.bfloat16
BY_LAST = (((1,), (1,)), ((), ()))
PLAIN = (((1,), (0,)), ((), ()))


def dot(a, b, contract=PLAIN):
    return lax.dot_general(a, b, contract, preferred_element_type=F32)


def kernel(
    nz, ny, nx,
    anc_ref, q_ref, k_ref, v_ref, g_ref, wq_ref, wk_ref, wv_ref, out_ref,
    w_all, kv_all, q_rows, g_rows, s_scr, p_scr, slots, stage, yrecv, zrecv, total,
    x_all, acc, sib_send, sib_recv, x_send, x_recv,
    w_sem, up_sem, side_sem, kv_sem, ys_sem, yr_sem, zs_sem, zr_sem,
    ss_sem, sr_sem, xs_sem, xr_sem,
):
    tok, q_width = q_ref.shape
    kv_width = k_ref.shape[1]
    kv_local = kv_width // HEAD_SIZE
    group = q_width // kv_width
    rows = group * tok
    n_slots = anc_ref.shape[1]
    deepest = n_slots - 1
    factor = HEAD_SIZE ** -0.5
    half_head = HEAD_SIZE // 2
    chunk = acc.shape[2]
    per = out_ref.shape[1] // chunk

    me, t = lax.axis_index("ctx"), lax.axis_index("tp")
    z, y = me // ny, me % ny
    x, core = t // 2, t % 2

    def remote(src, dst, send, recv, ctx, tp):
        return pltpu.make_async_remote_copy(
            src_ref=src, dst_ref=dst, send_sem=send, recv_sem=recv,
            device_id=(ctx, tp), device_id_type=MESH,
        )

    weights = (
        pltpu.make_async_copy(wq_ref, w_all.at[:, pl.ds(0, q_width)], w_sem.at[0]),
        pltpu.make_async_copy(wk_ref, w_all.at[:, pl.ds(q_width, kv_width)], w_sem.at[1]),
        pltpu.make_async_copy(wv_ref, w_all.at[:, pl.ds(q_width + kv_width, kv_width)], w_sem.at[2]),
    )
    for copy in weights:
        copy.start()

    barrier = pltpu.get_barrier_semaphore()

    def greet(ctx, tp):
        pl.semaphore_signal(barrier, inc=1, device_id=(ctx, tp), device_id_type=MESH)

    @pl.when(z > 0)
    def _():
        greet(me - ny, t)

    @pl.when(z < nz - 1)
    def _():
        greet(me + ny, t)

    for dy in range(1, ny):
        greet(z * ny + (y + dy) % ny, t)
    greet(me, x * 2 + 1 - core)
    for dx in range(1, nx):
        greet(me, ((x + dx) % nx) * 2 + core)
    kv_all[me, 0] = k_ref[...]
    kv_all[me, 1] = v_ref[...]
    peers = ny - 1 + nx + (z > 0).astype(jnp.int32) + (z < nz - 1).astype(jnp.int32)
    pl.semaphore_wait(barrier, peers)

    def up_copy(r, half):
        j = r * ny + y
        return remote(
            kv_all.at[j, half], kv_all.at[j, half], up_sem.at[r, half], kv_sem.at[j, half],
            me + ny, t,
        )

    def side_copy(r, yy, half):
        j = r * ny + y
        return remote(
            kv_all.at[j, half], kv_all.at[j, half], side_sem.at[r, yy, half], kv_sem.at[j, half],
            z * ny + yy, t,
        )

    def kv_arrival(j, half):
        remote(
            kv_all.at[j, half], kv_all.at[j, half], up_sem.at[0, half], kv_sem.at[j, half],
            me, t,
        ).wait_recv()

    for k in range(nz):
        r = z - k
        live = (r >= 0) & (r * ny + y != deepest)
        for half in range(2):
            if k > 0:
                @pl.when(live)
                def _():
                    kv_arrival(r * ny + y, half)

            @pl.when(live & (z < nz - 1))
            def _():
                up_copy(r, half).start()

            for dy in range(1, ny):
                yy = (y + dy) % ny

                @pl.when(live & ((k > 0) | (y < yy)))
                def _():
                    side_copy(r, yy, half).start()

        if k == 0:
            for h in range(kv_local):
                for g in range(group):
                    head = (h * group + g) * HEAD_SIZE
                    q_rows[h, g * tok:(g + 1) * tok, :] = q_ref[:, head:head + HEAD_SIZE]
                    g_rows[h, g * tok:(g + 1) * tok, :] = g_ref[:, head:head + HEAD_SIZE]
            depth = jnp.int32(0)
            for s in range(1, n_slots):
                depth += (anc_ref[me, s] != me).astype(jnp.int32)
            start = (depth * tok).astype(F32)
            scale = -2.0 * math.log(ROPE_BASE) / HEAD_SIZE
            which = lax.broadcasted_iota(jnp.int32, (half_head, tok), 0).astype(F32)
            place = lax.broadcasted_iota(jnp.int32, (half_head, tok), 1).astype(F32) + start
            angles = place * jnp.exp(which * scale)
            cos_t, sin_t = jnp.cos(angles), jnp.sin(angles)

    for k in range(nz):
        r = z - k
        for dy in range(1, ny):
            yy = (y + dy) % ny
            for half in range(2):
                @pl.when((r >= 0) & ((k > 0) | (yy < y)) & (r * ny + yy != deepest))
                def _():
                    kv_arrival(r * ny + yy, half)

    slots[n_slots] = jnp.zeros_like(slots[n_slots])
    power = factor * math.log2(math.e)
    key_id = lax.broadcasted_iota(jnp.int32, (tok, rows), 0)
    query_id = lax.broadcasted_iota(jnp.int32, (tok, rows), 1) % tok
    causal = key_id <= query_id
    for h in range(kv_local):
        cols = slice(h * HEAD_SIZE, (h + 1) * HEAD_SIZE)
        queries = q_rows[h]
        grads = g_rows[h]
        highest = jnp.full((1, rows), MASKED, F32)
        for s in range(n_slots):
            block = me if s == 0 else anc_ref[me, s]
            scores = dot(kv_all[block, 0, :, cols], queries, BY_LAST)
            if s == 0:
                scores = jnp.where(causal, scores, MASKED)
            else:
                scores = scores + jnp.where(block != me, 0.0, MASKED)
            s_scr[s] = scores
            highest = jnp.maximum(highest, jnp.max(scores, axis=0, keepdims=True))
            p_scr[s] = dot(kv_all[block, 1, :, cols], grads, BY_LAST)
        sums = jnp.zeros((1, rows), F32)
        dots = jnp.zeros((1, rows), F32)
        for s in range(n_slots):
            weights_s = jnp.exp2((s_scr[s] - highest) * power)
            s_scr[s] = weights_s
            sums = sums + jnp.sum(weights_s, axis=0, keepdims=True)
            dots = dots + jnp.sum(weights_s * p_scr[s], axis=0, keepdims=True)
        inverse = 1.0 / sums
        dots = dots * inverse
        query_grad = jnp.zeros((HEAD_SIZE, rows), F32)
        for s in range(n_slots):
            block = me if s == 0 else anc_ref[me, s]
            probs = s_scr[s] * inverse
            score_grads = (probs * (p_scr[s] - dots)).astype(BF16)
            slots[s, 0, :, cols] = (dot(score_grads, queries) * factor).astype(BF16)
            slots[s, 1, :, cols] = dot(probs.astype(BF16), grads).astype(BF16)
            keys_t = kv_all[block, 0, :, cols].T
            query_grad = query_grad + dot(keys_t, score_grads)
        query_grad = query_grad * factor
        for g in range(group):
            one = query_grad[:, g * tok:(g + 1) * tok]
            a, b = one[:half_head], one[half_head:]
            turned = jnp.concatenate([a * cos_t + b * sin_t, b * cos_t - a * sin_t], axis=0)
            head = (h * group + g) * HEAD_SIZE
            x_all[:, head:head + HEAD_SIZE] = turned.T.astype(BF16)

    def slot_of(j):
        found = jnp.int32(n_slots)
        for s in range(n_slots - 1, 0, -1):
            a = anc_ref[me, s]
            found = jnp.where((a == j) & (a != me), s, found)
        return jnp.where(j == me, 0, found)

    def y_copy(r, yy, half):
        return remote(
            stage.at[r * ny + yy, half], yrecv.at[r, y, half],
            ys_sem.at[r, yy, half], yr_sem.at[r, y, half], z * ny + yy, t,
        )

    def y_arrival(r, yy, half):
        remote(
            stage.at[r * ny + yy, half], yrecv.at[r, yy, half],
            ys_sem.at[r, yy, half], yr_sem.at[r, yy, half], me, t,
        ).wait_recv()

    def z_copy(r, half):
        return remote(
            stage.at[r * ny + y, half], zrecv.at[r, half],
            zs_sem.at[r, half], zr_sem.at[r, half], me - ny, t,
        )

    def y_sends(r, yy):
        return (r <= z) & ((r < z) | (yy < y)) & (r * ny + yy != deepest)

    for r in range(nz):
        for dy in range(1, ny):
            yy = (y + dy) % ny

            @pl.when(y_sends(r, yy))
            def _():
                j = r * ny + yy
                source = slot_of(j)
                for half in range(2):
                    stage[j, half] = slots[source, half]
                    y_copy(r, yy, half).start()

    for copy in weights:
        copy.wait()
    n_chunks = acc.shape[0]

    def query_part(i, carry):
        w = w_all[pl.ds(pl.multiple_of(i * chunk, chunk), chunk), pl.ds(0, q_width)]
        acc[i] = dot(x_all[:, 0:q_width], w, BY_LAST)
        return carry

    for r in range(nz):
        lax.fori_loop(n_chunks * r // nz, n_chunks * (r + 1) // nz, query_part, 0)

        @pl.when(r <= z)
        def _():
            j = r * ny + y
            source = slot_of(j)
            live = j != deepest
            for half in range(2):
                total[half] = slots[source, half].astype(F32)
                for dy in range(1, ny):
                    yy = (y + dy) % ny

                    @pl.when(live & ((r < z) | (y < yy)))
                    def _():
                        y_arrival(r, yy, half)
                        total[half] += yrecv[r, yy, half].astype(F32)

                @pl.when(live & (z < nz - 1))
                def _():
                    z_copy(r, half).wait_recv()
                    total[half] += zrecv[r, half].astype(F32)

                @pl.when(live & (r < z))
                def _():
                    stage[j, half] = total[half].astype(BF16)
                    z_copy(r, half).start()

    both_cos = jnp.concatenate([cos_t, cos_t], axis=0).T
    both_sin = jnp.concatenate([sin_t, -sin_t], axis=0).T
    for h in range(kv_local):
        one = total[0, :, h * HEAD_SIZE:(h + 1) * HEAD_SIZE]
        swapped = jnp.concatenate([one[:, half_head:], one[:, :half_head]], axis=1)
        at = q_width + h * HEAD_SIZE
        x_all[:, at:at + HEAD_SIZE] = (one * both_cos + swapped * both_sin).astype(BF16)
    x_all[:, q_width + kv_width:] = total[1].astype(BF16)

    def piece(target, i):
        at = target * per + i
        w = w_all[pl.ds(pl.multiple_of(at * chunk, chunk), chunk), pl.ds(q_width, 2 * kv_width)]
        return acc[at] + dot(x_all[:, q_width:], w, BY_LAST)

    def sib_copy(tx, i):
        return remote(
            sib_send.at[tx, i], sib_recv.at[tx, i], ss_sem.at[tx, i], sr_sem.at[tx, i],
            me, x * 2 + 1 - core,
        )

    def x_copy(tx, i):
        return remote(
            x_send.at[tx, i], x_recv.at[x, i], xs_sem.at[tx, i], xr_sem.at[x, i],
            me, tx * 2 + core,
        )

    def x_arrival(sx, i):
        remote(
            x_send.at[sx, i], x_recv.at[sx, i], xs_sem.at[sx, i], xr_sem.at[sx, i], me, t
        ).wait_recv()

    def to_sibling(tx):
        def body(i, carry):
            sib_send[tx, i] = piece(tx * 2 + 1 - core, i).astype(BF16)
            sib_copy(tx, i).start()
            return carry

        lax.fori_loop(0, per, body, 0)

    def from_sibling(tx, i):
        part = piece(tx * 2 + core, i)
        sib_copy(tx, i).wait_recv()
        return part + sib_recv[tx, i].astype(F32)

    for dx in range(1, nx):
        tx = (x + dx) % nx
        to_sibling(tx)

        def across(i, carry):
            x_send[tx, i] = from_sibling(tx, i).astype(BF16)
            x_copy(tx, i).start()
            return carry

        lax.fori_loop(0, per, across, 0)
    to_sibling(x)

    def last(i, carry):
        result = from_sibling(x, i)
        for dx in range(1, nx):
            sx = (x + dx) % nx
            x_arrival(sx, i)
            result = result + x_recv[sx, i].astype(F32)
        out_ref[:, pl.ds(pl.multiple_of(i * chunk, chunk), chunk)] = result.astype(BF16)
        return carry

    lax.fori_loop(0, per, last, 0)

    for k in range(nz):
        r = z - k
        live = (r >= 0) & (r * ny + y != deepest)
        for half in range(2):
            @pl.when(live & (z < nz - 1))
            def _():
                up_copy(r, half).wait_send()

            for dy in range(1, ny):
                yy = (y + dy) % ny

                @pl.when(live & ((k > 0) | (y < yy)))
                def _():
                    side_copy(r, yy, half).wait_send()
    for r in range(nz):
        for half in range(2):
            for dy in range(1, ny):
                yy = (y + dy) % ny

                @pl.when(y_sends(r, yy))
                def _():
                    y_copy(r, yy, half).wait_send()

            @pl.when((r < z) & (r * ny + y != deepest))
            def _():
                z_copy(r, half).wait_send()

    def drain(i, carry):
        for tx in range(nx):
            sib_copy(tx, i).wait_send()
        for dx in range(1, nx):
            x_copy((x + dx) % nx, i).wait_send()
        return carry

    lax.fori_loop(0, per, drain, 0)


def shards(nz, ny, nx, queries, keys, values, out_grad, ancestry, w_query, key_matrix, value_matrix):
    n = nz * ny
    tok, q_width = queries.shape
    kv_width = keys.shape[1]
    kv_local = kv_width // HEAD_SIZE
    rows = tok * (q_width // kv_width)
    model = w_query.shape[0]
    wide = model // (2 * nx)
    chunk = 256 if wide % 256 == 0 else 128
    per = wide // chunk
    n_slots = ancestry.shape[1]
    pair = (2, tok, kv_width)
    dma = pltpu.SemaphoreType.DMA
    vmem = pl.BlockSpec(memory_space=pltpu.VMEM)
    hbm = pl.BlockSpec(memory_space=pl.ANY)
    return pl.pallas_call(
        functools.partial(kernel, nz, ny, nx),
        out_shape=jax.ShapeDtypeStruct((tok, wide), BF16),
        in_specs=[pl.BlockSpec(memory_space=pltpu.SMEM), vmem, vmem, vmem, vmem, hbm, hbm, hbm],
        out_specs=vmem,
        scratch_shapes=[
            pltpu.VMEM((model, q_width + 2 * kv_width), BF16),
            pltpu.VMEM((n,) + pair, BF16),
            pltpu.VMEM((kv_local, rows, HEAD_SIZE), BF16),
            pltpu.VMEM((kv_local, rows, HEAD_SIZE), BF16),
            pltpu.VMEM((n_slots, tok, rows), F32),
            pltpu.VMEM((n_slots, tok, rows), F32),
            pltpu.VMEM((n_slots + 1,) + pair, BF16),
            pltpu.VMEM((n,) + pair, BF16),
            pltpu.VMEM((nz, ny) + pair, BF16),
            pltpu.VMEM((nz,) + pair, BF16),
            pltpu.VMEM(pair, F32),
            pltpu.VMEM((tok, q_width + 2 * kv_width), BF16),
            pltpu.VMEM((model // chunk, tok, chunk), F32),
            pltpu.VMEM((nx, per, tok, chunk), BF16),
            pltpu.VMEM((nx, per, tok, chunk), BF16),
            pltpu.VMEM((nx, per, tok, chunk), BF16),
            pltpu.VMEM((nx, per, tok, chunk), BF16),
            dma((3,)), dma((nz, 2)), dma((nz, ny, 2)), dma((n, 2)),
            dma((nz, ny, 2)), dma((nz, ny, 2)), dma((nz, 2)), dma((nz, 2)),
            dma((nx, per)), dma((nx, per)), dma((nx, per)), dma((nx, per)),
        ],
        compiler_params=pltpu.CompilerParams(
            collective_id=0, has_side_effects=True, vmem_limit_bytes=60 * 1024 * 1024
        ),
        name="tree_attention_backward",
    )(ancestry, queries, keys, values, out_grad, w_query, key_matrix, value_matrix)


def solution(mesh):
    n = mesh.shape["ctx"]
    ny = 2 ** ((n.bit_length() - 1) // 2)
    nx = mesh.shape["tp"] // 2
    in_specs = (
        P("ctx", "tp"),
        P("ctx", "tp"),
        P("ctx", "tp"),
        P("ctx", "tp"),
        P(),
        P(None, "tp"),
        P(None, "tp"),
        P(None, "tp"),
    )
    return jax.shard_map(
        functools.partial(shards, n // ny, ny, nx),
        mesh=mesh, in_specs=in_specs, out_specs=P("ctx", "tp"), check_vma=False,
    )
```

time: 238 us -> 58.4 us (0.25)
  waiting for transfers between devices: 94.8 us -> 0 us
  blocking collectives: 59.4 us -> 0 us
  Pallas kernels: 0 us -> 56.5 us
  matrix products: 31.1 us -> 0 us
  local copies, waits for them, and re-layouts: 27.6 us -> 1.72 us
  between operations: 13.6 us -> 0.01 us
  other arithmetic: 7.58 us -> 0 us
  loops' own time: 2.8 us -> 0 us
    unnamed x3 -> x0, waiting for transfers between devices: 69.1 us -> none
    all_gather x2 -> x0, blocking collectives: 59.4 us -> none  [the longest x1 30.8 us: shards(): lax.all_gather(keys, 'ctx', axis=0, tiled=True)]
    pallas_call x0 -> x1, Pallas kernels: none -> 56.5 us  [shards(): pl.pallas_call(functools.partial(kernel, nz, ny, nx), out_shape=jax.Shape...]
    dot_general x14 -> x0, matrix products: 31.1 us -> none  [the longest x1 10.7 us: shards(): lax.dot_general(query_low, w_query, contract, preferred_element_type=jnp....]
    reduce_scatter x1 -> x0, waiting for transfers between devices: 25.7 us -> none  [shards(): lax.psum_scatter(partial_sum.astype(jnp.bfloat16), 'tp', scatter_dimensio...]
    unnamed x19 -> x1, local copies, waits for them, and re-layouts: 9.69 us -> 1.72 us
    broadcast_in_dim x7 -> x0, local copies, waits for them, and re-layouts: 5.23 us -> none  [the longest x4 3.51 us: spread_mask(): jnp.broadcast_to(seen_mask[None, None], (kv_local, heads_per_group) + see...]
    dynamic_slice x2 -> x0, local copies, waits for them, and re-layouts: 3.57 us -> none  [turn(): lax.dynamic_slice_in_dim(values_all, offset, span_rows, 0)]
  transfers between devices with their start and end apart: 2 -> 0, of which waited for: 2 -> 0; matrix products, arithmetic and copies ran while one was open for 6% -> 0% of each run, Pallas kernels for 0% -> 0%
where the time goes in v1:
time: 58.4 us; the launch traced here: 58.3 us
  Pallas kernels  56.5 us (97%)
  local copies, waits for them, and re-layouts  1.72 us (3%)
    pallas_call x1, Pallas kernels, shards(): pl.pallas_call(functools.partial(kernel, nz, ny, nx), out_shape=jax.Shape...  56.5 us
    unnamed x1, local copies, waits for them, and re-layouts  1.72 us

profile of v1, /device:TPU:0, one launch (start us, length us, event | category | flops | bytes accessed | tf_op | source)
XLA Modules:
  0.0 58.3 jit_solution(16095086038831130477)
XLA Ops:
  0.0 56.5 %tree_attention_backward.1 = bf16[128,1280]{1,0:T(8,128)(2,1)} custom-call(s32[8,5]{1,0:T(8,128)} %anc_ref.1, bf16[128,1280]{1,0:T(8,128)(2,1)} %q_ref.1, bf16[128,256]{1,0:T(8,128)(2,1)} %k_ref.1, bf16[128,256]{1,0:T(8,128)(2,1)} %v_ref.1, bf16[128,1280]{1,0:T(8,128)(2,1)} %g_ref.1, bf16[5120,1280]{1,0:T(8,128)(2,1)} %wq_ref.1, bf16[5120,256]{1,0:T(8,128)(2,1)} %wk_ref.1, ...), custom_call_target="tpu_custom_call" | custom-call | tf_op jit(solution)/shard_map/tree_attention_backward/pallas_call | solution.py:393
  56.5 1.7 %copy.10 = bf16[128,1280]{1,0:T(8,128)(2,1)} copy(bf16[128,1280]{1,0:T(8,128)(2,1)} %tree_attention_backward.1) | data formatting | bytes 655360

commit v2 on v1

--- a/solution.py
+++ b/solution.py
@@ -25,7 +25,7 @@
 def kernel(
     nz, ny, nx,
     anc_ref, q_ref, k_ref, v_ref, g_ref, wq_ref, wk_ref, wv_ref, out_ref,
-    w_all, kv_all, q_rows, g_rows, s_scr, p_scr, slots, stage, yrecv, zrecv, total,
+    w_all, kv_all, q_rows, g_rows, s_scr, p_scr, stats, finals, turns, dq_acc, stage, yrecv, zrecv, total,
     x_all, acc, sib_send, sib_recv, x_send, x_recv,
     w_sem, up_sem, side_sem, kv_sem, ys_sem, yr_sem, zs_sem, zr_sem,
     ss_sem, sr_sem, xs_sem, xr_sem,
@@ -103,90 +103,183 @@
             me, t,
         ).wait_recv()
 
-    for k in range(nz):
+    power = factor * math.log2(math.e)
+    head_cols = [slice(h * HEAD_SIZE, (h + 1) * HEAD_SIZE) for h in range(kv_local)]
+
+    def forward(j, own):
+        for h, cols in enumerate(head_cols):
+            scores = dot(kv_all[j, 0, :, cols], q_rows[h], BY_LAST)
+            if own:
+                key_id = lax.broadcasted_iota(jnp.int32, (tok, rows), 0)
+                query_id = lax.broadcasted_iota(jnp.int32, (tok, rows), 1) % tok
+                scores = jnp.where(key_id <= query_id, scores, MASKED)
+            highest = jnp.max(scores, axis=0, keepdims=True)
+            raw = jnp.exp2((scores - highest) * power)
+            prob_grads = dot(kv_all[j, 1, :, cols], g_rows[h], BY_LAST)
+            s_scr[j, h] = raw
+            p_scr[j, h] = prob_grads
+            stats[j, h, 0:1] = highest
+            stats[j, h, 1:2] = jnp.sum(raw, axis=0, keepdims=True)
+            stats[j, h, 2:3] = jnp.sum(raw * prob_grads, axis=0, keepdims=True)
+
+    def start_block(r, half, first):
+        @pl.when((r * ny + y != deepest) & (z < nz - 1))
+        def _():
+            up_copy(r, half).start()
+
+        for dy in range(1, ny):
+            yy = (y + dy) % ny
+            later = (y < yy) if first else True
+
+            @pl.when((r * ny + y != deepest) & later)
+            def _():
+                side_copy(r, yy, half).start()
+
+    def from_sides(r):
+        for dy in range(1, ny):
+            yy = (y + dy) % ny
+
+            @pl.when(((r < z) | (yy < y)) & (r * ny + yy != deepest))
+            def _():
+                for half in range(2):
+                    kv_arrival(r * ny + yy, half)
+                forward(r * ny + yy, False)
+
+    for half in range(2):
+        start_block(z, half, True)
+    for h in range(kv_local):
+        for g in range(group):
+            head = (h * group + g) * HEAD_SIZE
+            q_rows[h, g * tok:(g + 1) * tok, :] = q_ref[:, head:head + HEAD_SIZE]
+            g_rows[h, g * tok:(g + 1) * tok, :] = g_ref[:, head:head + HEAD_SIZE]
+    depth = jnp.int32(0)
+    for s in range(1, n_slots):
+        depth += (anc_ref[me, s] != me).astype(jnp.int32)
+    start = (depth * tok).astype(F32)
+    scale = -2.0 * math.log(ROPE_BASE) / HEAD_SIZE
+    which = lax.broadcasted_iota(jnp.int32, (half_head, tok), 0).astype(F32)
+    place = lax.broadcasted_iota(jnp.int32, (half_head, tok), 1).astype(F32) + start
+    angles = place * jnp.exp(which * scale)
+    turns[0], turns[1] = jnp.cos(angles), jnp.sin(angles)
+    dq_acc[...] = jnp.zeros_like(dq_acc)
+    for j in range(nz * ny):
+        stats[j, :, 0:1] = jnp.full((kv_local, 1, rows), MASKED, F32)
+        stats[j, :, 1:3] = jnp.zeros((kv_local, 2, rows), F32)
+    forward(me, True)
+
+    def gather_step(k, carry):
         r = z - k
-        live = (r >= 0) & (r * ny + y != deepest)
+
+        @pl.when(r * ny + y != deepest)
+        def _():
+            for half in range(2):
+                kv_arrival(r * ny + y, half)
+                start_block(r, half, False)
+            forward(r * ny + y, False)
+
+        from_sides(r + 1)
+        return carry
+
+    lax.fori_loop(1, z + 1, gather_step, 0)
+    from_sides(jnp.int32(0))
+
+    shifts = []
+    for j in range(nz * ny):
+        seen = me == j
+        for s in range(1, n_slots):
+            seen = seen | (anc_ref[me, s] == j)
+        shifts.append(jnp.where(seen, 0.0, MASKED))
+    for h in range(kv_local):
+        highest = jnp.full((1, rows), MASKED, F32)
+        for j in range(nz * ny):
+            highest = jnp.maximum(highest, stats[j, h, 0:1] + shifts[j])
+        sums = jnp.zeros((1, rows), F32)
+        dots = jnp.zeros((1, rows), F32)
+        for j in range(nz * ny):
+            shrink = jnp.exp2((stats[j, h, 0:1] + shifts[j] - highest) * power)
+            stats[j, h, 0:1] = shrink
+            sums = sums + shrink * stats[j, h, 1:2]
+            dots = dots + shrink * stats[j, h, 2:3]
+        inverse = 1.0 / sums
+        finals[h, 0:1] = inverse
+        finals[h, 1:2] = dots * inverse
+
+    def y_copy(r, yy, half):
+        return remote(
+            stage.at[r * ny + yy, half], yrecv.at[r, y, half],
+            ys_sem.at[r, yy, half], yr_sem.at[r, y, half], z * ny + yy, t,
+        )
+
+    def y_arrival(r, yy, half):
+        remote(
+            stage.at[r * ny + yy, half], yrecv.at[r, yy, half],
+            ys_sem.at[r, yy, half], yr_sem.at[r, yy, half], me, t,
+        ).wait_recv()
+
+    def z_copy(r, half):
+        return remote(
+            stage.at[r * ny + y, half], zrecv.at[r, half],
+            zs_sem.at[r, half], zr_sem.at[r, half], me - ny, t,
+        )
+
+    def y_sends(r, yy):
+        return (r <= z) & ((r < z) | (yy < y)) & (r * ny + yy != deepest)
+
+    def backward(j):
+        for h, cols in enumerate(head_cols):
+            probs = s_scr[j, h] * (stats[j, h, 0:1] * finals[h, 0:1])
+            score_grads = (probs * (p_scr[j, h] - finals[h, 1:2])).astype(BF16)
+            stage[j, 0, :, cols] = (dot(score_grads, q_rows[h]) * factor).astype(BF16)
+            stage[j, 1, :, cols] = dot(probs.astype(BF16), g_rows[h]).astype(BF16)
+            dq_acc[h] += dot(kv_all[j, 0, :, cols].T, score_grads)
+
+    def chain(r):
+        j = r * ny + y
+        live = j != deepest
         for half in range(2):
-            if k > 0:
-                @pl.when(live)
-                def _():
-                    kv_arrival(r * ny + y, half)
-
-            @pl.when(live & (z < nz - 1))
-            def _():
-                up_copy(r, half).start()
-
+            total[half] = stage[j, half].astype(F32)
             for dy in range(1, ny):
                 yy = (y + dy) % ny
 
-                @pl.when(live & ((k > 0) | (y < yy)))
+                @pl.when(live & ((r < z) | (y < yy)))
                 def _():
-                    side_copy(r, yy, half).start()
-
-        if k == 0:
-            for h in range(kv_local):
-                for g in range(group):
-                    head = (h * group + g) * HEAD_SIZE
-                    q_rows[h, g * tok:(g + 1) * tok, :] = q_ref[:, head:head + HEAD_SIZE]
-                    g_rows[h, g * tok:(g + 1) * tok, :] = g_ref[:, head:head + HEAD_SIZE]
-            depth = jnp.int32(0)
-            for s in range(1, n_slots):
-                depth += (anc_ref[me, s] != me).astype(jnp.int32)
-            start = (depth * tok).astype(F32)
-            scale = -2.0 * math.log(ROPE_BASE) / HEAD_SIZE
-            which = lax.broadcasted_iota(jnp.int32, (half_head, tok), 0).astype(F32)
-            place = lax.broadcasted_iota(jnp.int32, (half_head, tok), 1).astype(F32) + start
-            angles = place * jnp.exp(which * scale)
-            cos_t, sin_t = jnp.cos(angles), jnp.sin(angles)
-
-    for k in range(nz):
-        r = z - k
+                    y_arrival(r, yy, half)
+                    total[half] += yrecv[r, yy, half].astype(F32)
+
+            @pl.when(live & (z < nz - 1))
+            def _():
+                z_copy(r, half).wait_recv()
+                total[half] += zrecv[r, half].astype(F32)
+
+            @pl.when(live & (r < z))
+            def _():
+                stage[j, half] = total[half].astype(BF16)
+                z_copy(r, half).start()
+
+    def back_step(r, carry):
         for dy in range(1, ny):
             yy = (y + dy) % ny
-            for half in range(2):
-                @pl.when((r >= 0) & ((k > 0) | (yy < y)) & (r * ny + yy != deepest))
-                def _():
-                    kv_arrival(r * ny + yy, half)
-
-    slots[n_slots] = jnp.zeros_like(slots[n_slots])
-    power = factor * math.log2(math.e)
-    key_id = lax.broadcasted_iota(jnp.int32, (tok, rows), 0)
-    query_id = lax.broadcasted_iota(jnp.int32, (tok, rows), 1) % tok
-    causal = key_id <= query_id
+
+            @pl.when(y_sends(r, yy))
+            def _():
+                backward(r * ny + yy)
+                for half in range(2):
+                    y_copy(r, yy, half).start()
+
+        @pl.when((r * ny + y != deepest) | (r == z))
+        def _():
+            backward(r * ny + y)
+
+        @pl.when((z == nz - 1) & (r > 0) & ((r - 1) * ny + y != deepest))
+        def _():
+            chain(r - 1)
+
+        return carry
+
+    lax.fori_loop(0, z + 1, back_step, 0)
+    cos_t, sin_t = turns[0], turns[1]
     for h in range(kv_local):
-        cols = slice(h * HEAD_SIZE, (h + 1) * HEAD_SIZE)
-        queries = q_rows[h]
-        grads = g_rows[h]
-        highest = jnp.full((1, rows), MASKED, F32)
-        for s in range(n_slots):
-            block = me if s == 0 else anc_ref[me, s]
-            scores = dot(kv_all[block, 0, :, cols], queries, BY_LAST)
-            if s == 0:
-                scores = jnp.where(causal, scores, MASKED)
-            else:
-                scores = scores + jnp.where(block != me, 0.0, MASKED)
-            s_scr[s] = scores
-            highest = jnp.maximum(highest, jnp.max(scores, axis=0, keepdims=True))
-            p_scr[s] = dot(kv_all[block, 1, :, cols], grads, BY_LAST)
-        sums = jnp.zeros((1, rows), F32)
-        dots = jnp.zeros((1, rows), F32)
-        for s in range(n_slots):
-            weights_s = jnp.exp2((s_scr[s] - highest) * power)
-            s_scr[s] = weights_s
-            sums = sums + jnp.sum(weights_s, axis=0, keepdims=True)
-            dots = dots + jnp.sum(weights_s * p_scr[s], axis=0, keepdims=True)
-        inverse = 1.0 / sums
-        dots = dots * inverse
-        query_grad = jnp.zeros((HEAD_SIZE, rows), F32)
-        for s in range(n_slots):
-            block = me if s == 0 else anc_ref[me, s]
-            probs = s_scr[s] * inverse
-            score_grads = (probs * (p_scr[s] - dots)).astype(BF16)
-            slots[s, 0, :, cols] = (dot(score_grads, queries) * factor).astype(BF16)
-            slots[s, 1, :, cols] = dot(probs.astype(BF16), grads).astype(BF16)
-            keys_t = kv_all[block, 0, :, cols].T
-            query_grad = query_grad + dot(keys_t, score_grads)
-        query_grad = query_grad * factor
+        query_grad = dq_acc[h] * factor
         for g in range(group):
             one = query_grad[:, g * tok:(g + 1) * tok]
             a, b = one[:half_head], one[half_head:]
@@ -194,46 +287,6 @@
             head = (h * group + g) * HEAD_SIZE
             x_all[:, head:head + HEAD_SIZE] = turned.T.astype(BF16)
 
-    def slot_of(j):
-        found = jnp.int32(n_slots)
-        for s in range(n_slots - 1, 0, -1):
-            a = anc_ref[me, s]
-            found = jnp.where((a == j) & (a != me), s, found)
-        return jnp.where(j == me, 0, found)
-
-    def y_copy(r, yy, half):
-        return remote(
-            stage.at[r * ny + yy, half], yrecv.at[r, y, half],
-            ys_sem.at[r, yy, half], yr_sem.at[r, y, half], z * ny + yy, t,
-        )
-
-    def y_arrival(r, yy, half):
-        remote(
-            stage.at[r * ny + yy, half], yrecv.at[r, yy, half],
-            ys_sem.at[r, yy, half], yr_sem.at[r, yy, half], me, t,
-        ).wait_recv()
-
-    def z_copy(r, half):
-        return remote(
-            stage.at[r * ny + y, half], zrecv.at[r, half],
-            zs_sem.at[r, half], zr_sem.at[r, half], me - ny, t,
-        )
-
-    def y_sends(r, yy):
-        return (r <= z) & ((r < z) | (yy < y)) & (r * ny + yy != deepest)
-
-    for r in range(nz):
-        for dy in range(1, ny):
-            yy = (y + dy) % ny
-
-            @pl.when(y_sends(r, yy))
-            def _():
-                j = r * ny + yy
-                source = slot_of(j)
-                for half in range(2):
-                    stage[j, half] = slots[source, half]
-                    y_copy(r, yy, half).start()
-
     for copy in weights:
         copy.wait()
     n_chunks = acc.shape[0]
@@ -243,33 +296,20 @@
         acc[i] = dot(x_all[:, 0:q_width], w, BY_LAST)
         return carry
 
-    for r in range(nz):
-        lax.fori_loop(n_chunks * r // nz, n_chunks * (r + 1) // nz, query_part, 0)
-
-        @pl.when(r <= z)
+    first_left = jnp.where(z == nz - 1, z, 0)
+
+    def chain_step(r, carry):
+        count = z + 1 - first_left
+        at = r - first_left
+        lax.fori_loop(n_chunks * at // count, n_chunks * (at + 1) // count, query_part, 0)
+
+        @pl.when((r * ny + y != deepest) | (r == z))
         def _():
-            j = r * ny + y
-            source = slot_of(j)
-            live = j != deepest
-            for half in range(2):
-                total[half] = slots[source, half].astype(F32)
-                for dy in range(1, ny):
-                    yy = (y + dy) % ny
-
-                    @pl.when(live & ((r < z) | (y < yy)))
-                    def _():
-                        y_arrival(r, yy, half)
-                        total[half] += yrecv[r, yy, half].astype(F32)
-
-                @pl.when(live & (z < nz - 1))
-                def _():
-                    z_copy(r, half).wait_recv()
-                    total[half] += zrecv[r, half].astype(F32)
-
-                @pl.when(live & (r < z))
-                def _():
-                    stage[j, half] = total[half].astype(BF16)
-                    z_copy(r, half).start()
+            chain(r)
+
+        return carry
+
+    lax.fori_loop(first_left, z + 1, chain_step, 0)
 
     both_cos = jnp.concatenate([cos_t, cos_t], axis=0).T
     both_sin = jnp.concatenate([sin_t, -sin_t], axis=0).T
@@ -385,7 +425,6 @@
     wide = model // (2 * nx)
     chunk = 256 if wide % 256 == 0 else 128
     per = wide // chunk
-    n_slots = ancestry.shape[1]
     pair = (2, tok, kv_width)
     dma = pltpu.SemaphoreType.DMA
     vmem = pl.BlockSpec(memory_space=pltpu.VMEM)
@@ -400,9 +439,12 @@
             pltpu.VMEM((n,) + pair, BF16),
             pltpu.VMEM((kv_local, rows, HEAD_SIZE), BF16),
             pltpu.VMEM((kv_local, rows, HEAD_SIZE), BF16),
-            pltpu.VMEM((n_slots, tok, rows), F32),
-            pltpu.VMEM((n_slots, tok, rows), F32),
-            pltpu.VMEM((n_slots + 1,) + pair, BF16),
+            pltpu.VMEM((n, kv_local, tok, rows), F32),
+            pltpu.VMEM((n, kv_local, tok, rows), F32),
+            pltpu.VMEM((n, kv_local, 8, rows), F32),
+            pltpu.VMEM((kv_local, 8, rows), F32),
+            pltpu.VMEM((2, HEAD_SIZE // 2, tok), F32),
+            pltpu.VMEM((kv_local, HEAD_SIZE, rows), F32),
             pltpu.VMEM((n,) + pair, BF16),
             pltpu.VMEM((nz, ny) + pair, BF16),
             pltpu.VMEM((nz,) + pair, BF16),

time: 58.4 us -> 49 us (0.84)
  Pallas kernels: 56.5 us -> 47.1 us
    pallas_call x1, Pallas kernels: 56.5 us -> 47.1 us  [shards(): pl.pallas_call(functools.partial(kernel, nz, ny, nx), out_shape=jax.Shape...]
where the time goes in v2:
time: 49 us; the launch traced here: 48.8 us
  Pallas kernels  47.1 us (96%)
  local copies, waits for them, and re-layouts  1.72 us (4%)
    pallas_call x1, Pallas kernels, shards(): pl.pallas_call(functools.partial(kernel, nz, ny, nx), out_shape=jax.Shape...  47.1 us
    unnamed x1, local copies, waits for them, and re-layouts  1.72 us

profile of v2, /device:TPU:0, one launch (start us, length us, event | category | flops | bytes accessed | tf_op | source)
XLA Modules:
  0.0 48.8 jit_solution(17864344039131146666)
XLA Ops:
  0.0 47.1 %tree_attention_backward.1 = bf16[128,1280]{1,0:T(8,128)(2,1)} custom-call(s32[8,5]{1,0:T(8,128)} %anc_ref.1, bf16[128,1280]{1,0:T(8,128)(2,1)} %q_ref.1, bf16[128,256]{1,0:T(8,128)(2,1)} %k_ref.1, bf16[128,256]{1,0:T(8,128)(2,1)} %v_ref.1, bf16[128,1280]{1,0:T(8,128)(2,1)} %g_ref.1, bf16[5120,1280]{1,0:T(8,128)(2,1)} %wq_ref.1, bf16[5120,256]{1,0:T(8,128)(2,1)} %wk_ref.1, ...), custom_call_target="tpu_custom_call" | custom-call | tf_op jit(solution)/shard_map/tree_attention_backward/pallas_call | solution.py:432
  47.1 1.7 %copy.10 = bf16[128,1280]{1,0:T(8,128)(2,1)} copy(bf16[128,1280]{1,0:T(8,128)(2,1)} %tree_attention_backward.1) | data formatting | bytes 655360

commit v3 on v2

--- a/solution.py
+++ b/solution.py
@@ -27,7 +27,7 @@
     anc_ref, q_ref, k_ref, v_ref, g_ref, wq_ref, wk_ref, wv_ref, out_ref,
     w_all, kv_all, q_rows, g_rows, s_scr, p_scr, stats, finals, turns, dq_acc, stage, yrecv, zrecv, total,
     x_all, acc, sib_send, sib_recv, x_send, x_recv,
-    w_sem, up_sem, side_sem, kv_sem, ys_sem, yr_sem, zs_sem, zr_sem,
+    w_sem, row_sem, up_sem, side_sem, kv_sem, ys_sem, yr_sem, zs_sem, zr_sem,
     ss_sem, sr_sem, xs_sem, xr_sem,
 ):
     tok, q_width = q_ref.shape
@@ -57,7 +57,23 @@
         pltpu.make_async_copy(wk_ref, w_all.at[:, pl.ds(q_width, kv_width)], w_sem.at[1]),
         pltpu.make_async_copy(wv_ref, w_all.at[:, pl.ds(q_width + kv_width, kv_width)], w_sem.at[2]),
     )
-    for copy in weights:
+    own_kv = (
+        pltpu.make_async_copy(k_ref, kv_all.at[me, 0], w_sem.at[3]),
+        pltpu.make_async_copy(v_ref, kv_all.at[me, 1], w_sem.at[4]),
+    )
+    row_copies = []
+    for h in range(kv_local):
+        for g in range(group):
+            head = h * group + g
+            for side, (src, dst) in enumerate(((q_ref, q_rows), (g_ref, g_rows))):
+                row_copies.append(
+                    pltpu.make_async_copy(
+                        src.at[:, pl.ds(head * HEAD_SIZE, HEAD_SIZE)],
+                        dst.at[h, pl.ds(g * tok, tok)],
+                        row_sem.at[side, head],
+                    )
+                )
+    for copy in (*own_kv, *row_copies, *weights):
         copy.start()
 
     barrier = pltpu.get_barrier_semaphore()
@@ -65,23 +81,16 @@
     def greet(ctx, tp):
         pl.semaphore_signal(barrier, inc=1, device_id=(ctx, tp), device_id_type=MESH)
 
-    @pl.when(z > 0)
-    def _():
-        greet(me - ny, t)
-
-    @pl.when(z < nz - 1)
-    def _():
-        greet(me + ny, t)
-
+    for dz in range(1, nz):
+        greet(((z + dz) % nz) * ny + y, t)
     for dy in range(1, ny):
         greet(z * ny + (y + dy) % ny, t)
     greet(me, x * 2 + 1 - core)
     for dx in range(1, nx):
         greet(me, ((x + dx) % nx) * 2 + core)
-    kv_all[me, 0] = k_ref[...]
-    kv_all[me, 1] = v_ref[...]
-    peers = ny - 1 + nx + (z > 0).astype(jnp.int32) + (z < nz - 1).astype(jnp.int32)
-    pl.semaphore_wait(barrier, peers)
+    pl.semaphore_wait(barrier, nz - 1 + ny - 1 + 1 + nx - 1)
+    for copy in own_kv:
+        copy.wait()
 
     def up_copy(r, half):
         j = r * ny + y
@@ -147,11 +156,6 @@
 
     for half in range(2):
         start_block(z, half, True)
-    for h in range(kv_local):
-        for g in range(group):
-            head = (h * group + g) * HEAD_SIZE
-            q_rows[h, g * tok:(g + 1) * tok, :] = q_ref[:, head:head + HEAD_SIZE]
-            g_rows[h, g * tok:(g + 1) * tok, :] = g_ref[:, head:head + HEAD_SIZE]
     depth = jnp.int32(0)
     for s in range(1, n_slots):
         depth += (anc_ref[me, s] != me).astype(jnp.int32)
@@ -165,6 +169,8 @@
     for j in range(nz * ny):
         stats[j, :, 0:1] = jnp.full((kv_local, 1, rows), MASKED, F32)
         stats[j, :, 1:3] = jnp.zeros((kv_local, 2, rows), F32)
+    for copy in row_copies:
+        copy.wait()
     forward(me, True)
 
     def gather_step(k, carry):
@@ -218,9 +224,15 @@
 
     def z_copy(r, half):
         return remote(
-            stage.at[r * ny + y, half], zrecv.at[r, half],
-            zs_sem.at[r, half], zr_sem.at[r, half], me - ny, t,
-        )
+            stage.at[r * ny + y, half], zrecv.at[z, half],
+            zs_sem.at[r, half], zr_sem.at[z, half], r * ny + y, t,
+        )
+
+    def z_arrival(sz, half):
+        remote(
+            stage.at[me, half], zrecv.at[sz, half],
+            zs_sem.at[sz, half], zr_sem.at[sz, half], me, t,
+        ).wait_recv()
 
     def y_sends(r, yy):
         return (r <= z) & ((r < z) | (yy < y)) & (r * ny + yy != deepest)
@@ -246,11 +258,6 @@
                     y_arrival(r, yy, half)
                     total[half] += yrecv[r, yy, half].astype(F32)
 
-            @pl.when(live & (z < nz - 1))
-            def _():
-                z_copy(r, half).wait_recv()
-                total[half] += zrecv[r, half].astype(F32)
-
             @pl.when(live & (r < z))
             def _():
                 stage[j, half] = total[half].astype(BF16)
@@ -270,7 +277,7 @@
         def _():
             backward(r * ny + y)
 
-        @pl.when((z == nz - 1) & (r > 0) & ((r - 1) * ny + y != deepest))
+        @pl.when((r > 0) & ((r - 1) * ny + y != deepest))
         def _():
             chain(r - 1)
 
@@ -292,24 +299,23 @@
     n_chunks = acc.shape[0]
 
     def query_part(i, carry):
-        w = w_all[pl.ds(pl.multiple_of(i * chunk, chunk), chunk), pl.ds(0, q_width)]
-        acc[i] = dot(x_all[:, 0:q_width], w, BY_LAST)
-        return carry
-
-    first_left = jnp.where(z == nz - 1, z, 0)
-
-    def chain_step(r, carry):
-        count = z + 1 - first_left
-        at = r - first_left
-        lax.fori_loop(n_chunks * at // count, n_chunks * (at + 1) // count, query_part, 0)
-
-        @pl.when((r * ny + y != deepest) | (r == z))
-        def _():
-            chain(r)
-
-        return carry
-
-    lax.fori_loop(first_left, z + 1, chain_step, 0)
+        tx = (x + 1 + i // (2 * per)) % nx
+        at = tx * (2 * per) + i % (2 * per)
+        w = w_all[pl.ds(pl.multiple_of(at * chunk, chunk), chunk), pl.ds(0, q_width)]
+        acc[at] = dot(x_all[:, 0:q_width], w, BY_LAST)
+        return carry
+
+    early = jnp.where(z == nz - 1, n_chunks - 2 * per, n_chunks)
+    lax.fori_loop(0, early, query_part, 0)
+    chain(z)
+
+    def from_above(sz, carry):
+        for half in range(2):
+            z_arrival(sz, half)
+            total[half] += zrecv[sz, half].astype(F32)
+        return carry
+
+    lax.fori_loop(z + 1, jnp.where(me == deepest, z + 1, nz), from_above, 0)
 
     both_cos = jnp.concatenate([cos_t, cos_t], axis=0).T
     both_sin = jnp.concatenate([sin_t, -sin_t], axis=0).T
@@ -365,6 +371,7 @@
             return carry
 
         lax.fori_loop(0, per, across, 0)
+    lax.fori_loop(early, n_chunks, query_part, 0)
     to_sibling(x)
 
     def last(i, carry):
@@ -432,7 +439,7 @@
     return pl.pallas_call(
         functools.partial(kernel, nz, ny, nx),
         out_shape=jax.ShapeDtypeStruct((tok, wide), BF16),
-        in_specs=[pl.BlockSpec(memory_space=pltpu.SMEM), vmem, vmem, vmem, vmem, hbm, hbm, hbm],
+        in_specs=[pl.BlockSpec(memory_space=pltpu.SMEM)] + [hbm] * 7,
         out_specs=vmem,
         scratch_shapes=[
             pltpu.VMEM((model, q_width + 2 * kv_width), BF16),
@@ -455,7 +462,7 @@
             pltpu.VMEM((nx, per, tok, chunk), BF16),
             pltpu.VMEM((nx, per, tok, chunk), BF16),
             pltpu.VMEM((nx, per, tok, chunk), BF16),
-            dma((3,)), dma((nz, 2)), dma((nz, ny, 2)), dma((n, 2)),
+            dma((5,)), dma((2, q_width // HEAD_SIZE)), dma((nz, 2)), dma((nz, ny, 2)), dma((n, 2)),
             dma((nz, ny, 2)), dma((nz, ny, 2)), dma((nz, 2)), dma((nz, 2)),
             dma((nx, per)), dma((nx, per)), dma((nx, per)), dma((nx, per)),
         ],

time: 49 us -> 46 us (0.939)
  the two profiles are of different devices: /device:TPU:0 before, /device:TPU:20 now
where the time goes in v3:
time: 46 us; the launch traced here: 45.8 us
  Pallas kernels  44.1 us (96%)
  local copies, waits for them, and re-layouts  1.72 us (4%)
    pallas_call x1, Pallas kernels, shards(): pl.pallas_call(functools.partial(kernel, nz, ny, nx), out_shape=jax.Shape...  44.1 us
    unnamed x1, local copies, waits for them, and re-layouts  1.72 us

profile of v3, /device:TPU:20, one launch (start us, length us, event | category | flops | bytes accessed | tf_op | source)
XLA Modules:
  0.0 45.8 jit_solution(7797572471304010723)
XLA Ops:
  0.0 44.1 %tree_attention_backward.1 = bf16[128,1280]{1,0:T(8,128)(2,1)} custom-call(s32[8,5]{1,0:T(8,128)} %anc_ref.1, bf16[128,1280]{1,0:T(8,128)(2,1)} %q_ref.1, bf16[128,256]{1,0:T(8,128)(2,1)} %k_ref.1, bf16[128,256]{1,0:T(8,128)(2,1)} %v_ref.1, bf16[128,1280]{1,0:T(8,128)(2,1)} %g_ref.1, bf16[5120,1280]{1,0:T(8,128)(2,1)} %wq_ref.1, bf16[5120,256]{1,0:T(8,128)(2,1)} %wk_ref.1, ...), custom_call_target="tpu_custom_call" | custom-call | tf_op jit(solution)/shard_map/tree_attention_backward/pallas_call | solution.py:439
  44.1 1.7 %copy.10 = bf16[128,1280]{1,0:T(8,128)(2,1)} copy(bf16[128,1280]{1,0:T(8,128)(2,1)} %tree_attention_backward.1) | data formatting | bytes 655360

commit v4 on v3

--- a/solution.py
+++ b/solution.py
@@ -26,7 +26,7 @@
     nz, ny, nx,
     anc_ref, q_ref, k_ref, v_ref, g_ref, wq_ref, wk_ref, wv_ref, out_ref,
     w_all, kv_all, q_rows, g_rows, s_scr, p_scr, stats, finals, turns, dq_acc, stage, yrecv, zrecv, total,
-    x_all, acc, sib_send, sib_recv, x_send, x_recv,
+    x_t, acc, sib_send, sib_recv, x_send, x_recv,
     w_sem, row_sem, up_sem, side_sem, kv_sem, ys_sem, yr_sem, zs_sem, zr_sem,
     ss_sem, sr_sem, xs_sem, xr_sem,
 ):
@@ -39,8 +39,9 @@
     deepest = n_slots - 1
     factor = HEAD_SIZE ** -0.5
     half_head = HEAD_SIZE // 2
-    chunk = acc.shape[2]
-    per = out_ref.shape[1] // chunk
+    chunk = sib_send.shape[2]
+    wide = out_ref.shape[1]
+    per = wide // chunk
 
     me, t = lax.axis_index("ctx"), lax.axis_index("tp")
     z, y = me // ny, me % ny
@@ -292,20 +293,19 @@
             a, b = one[:half_head], one[half_head:]
             turned = jnp.concatenate([a * cos_t + b * sin_t, b * cos_t - a * sin_t], axis=0)
             head = (h * group + g) * HEAD_SIZE
-            x_all[:, head:head + HEAD_SIZE] = turned.T.astype(BF16)
+            x_t[head:head + HEAD_SIZE, :] = turned.astype(BF16)
 
     for copy in weights:
         copy.wait()
-    n_chunks = acc.shape[0]
+    def quarter_at(target):
+        return pl.ds(pl.multiple_of(target * wide, HEAD_SIZE), wide)
 
     def query_part(i, carry):
-        tx = (x + 1 + i // (2 * per)) % nx
-        at = tx * (2 * per) + i % (2 * per)
-        w = w_all[pl.ds(pl.multiple_of(at * chunk, chunk), chunk), pl.ds(0, q_width)]
-        acc[at] = dot(x_all[:, 0:q_width], w, BY_LAST)
-        return carry
-
-    early = jnp.where(z == nz - 1, n_chunks - 2 * per, n_chunks)
+        at = quarter_at(((x + 1 + i // 2) % nx) * 2 + i % 2)
+        acc[at] = dot(w_all[at, 0:q_width], x_t[0:q_width])
+        return carry
+
+    early = jnp.where(z == nz - 1, 2 * nx - 2, 2 * nx)
     lax.fori_loop(0, early, query_part, 0)
     chain(z)
 
@@ -317,19 +317,21 @@
 
     lax.fori_loop(z + 1, jnp.where(me == deepest, z + 1, nz), from_above, 0)
 
-    both_cos = jnp.concatenate([cos_t, cos_t], axis=0).T
-    both_sin = jnp.concatenate([sin_t, -sin_t], axis=0).T
-    for h in range(kv_local):
-        one = total[0, :, h * HEAD_SIZE:(h + 1) * HEAD_SIZE]
-        swapped = jnp.concatenate([one[:, half_head:], one[:, :half_head]], axis=1)
+    for h, cols in enumerate(head_cols):
+        one = total[0, :, cols].T
+        a, b = one[:half_head], one[half_head:]
+        turned = jnp.concatenate([a * cos_t + b * sin_t, b * cos_t - a * sin_t], axis=0)
         at = q_width + h * HEAD_SIZE
-        x_all[:, at:at + HEAD_SIZE] = (one * both_cos + swapped * both_sin).astype(BF16)
-    x_all[:, q_width + kv_width:] = total[1].astype(BF16)
+        x_t[at:at + HEAD_SIZE, :] = turned.astype(BF16)
+        at = at + kv_width
+        x_t[at:at + HEAD_SIZE, :] = total[1, :, cols].T.astype(BF16)
+
+    def key_value_part(target):
+        at = quarter_at(target)
+        acc[at] += dot(w_all[at, q_width:], x_t[q_width:])
 
     def piece(target, i):
-        at = target * per + i
-        w = w_all[pl.ds(pl.multiple_of(at * chunk, chunk), chunk), pl.ds(q_width, 2 * kv_width)]
-        return acc[at] + dot(x_all[:, q_width:], w, BY_LAST)
+        return acc[pl.ds(pl.multiple_of(target * wide + i * chunk, HEAD_SIZE), chunk)]
 
     def sib_copy(tx, i):
         return remote(
@@ -349,6 +351,8 @@
         ).wait_recv()
 
     def to_sibling(tx):
+        key_value_part(tx * 2 + 1 - core)
+
         def body(i, carry):
             sib_send[tx, i] = piece(tx * 2 + 1 - core, i).astype(BF16)
             sib_copy(tx, i).start()
@@ -364,6 +368,7 @@
     for dx in range(1, nx):
         tx = (x + dx) % nx
         to_sibling(tx)
+        key_value_part(tx * 2 + core)
 
         def across(i, carry):
             x_send[tx, i] = from_sibling(tx, i).astype(BF16)
@@ -371,8 +376,9 @@
             return carry
 
         lax.fori_loop(0, per, across, 0)
-    lax.fori_loop(early, n_chunks, query_part, 0)
+    lax.fori_loop(early, 2 * nx, query_part, 0)
     to_sibling(x)
+    key_value_part(x * 2 + core)
 
     def last(i, carry):
         result = from_sibling(x, i)
@@ -380,7 +386,7 @@
             sx = (x + dx) % nx
             x_arrival(sx, i)
             result = result + x_recv[sx, i].astype(F32)
-        out_ref[:, pl.ds(pl.multiple_of(i * chunk, chunk), chunk)] = result.astype(BF16)
+        out_ref[:, pl.ds(pl.multiple_of(i * chunk, chunk), chunk)] = result.T.astype(BF16)
         return carry
 
     lax.fori_loop(0, per, last, 0)
@@ -456,12 +462,12 @@
             pltpu.VMEM((nz, ny) + pair, BF16),
             pltpu.VMEM((nz,) + pair, BF16),
             pltpu.VMEM(pair, F32),
-            pltpu.VMEM((tok, q_width + 2 * kv_width), BF16),
-            pltpu.VMEM((model // chunk, tok, chunk), F32),
-            pltpu.VMEM((nx, per, tok, chunk), BF16),
-            pltpu.VMEM((nx, per, tok, chunk), BF16),
-            pltpu.VMEM((nx, per, tok, chunk), BF16),
-            pltpu.VMEM((nx, per, tok, chunk), BF16),
+            pltpu.VMEM((q_width + 2 * kv_width, tok), BF16),
+            pltpu.VMEM((model, tok), F32),
+            pltpu.VMEM((nx, per, chunk, tok), BF16),
+            pltpu.VMEM((nx, per, chunk, tok), BF16),
+            pltpu.VMEM((nx, per, chunk, tok), BF16),
+            pltpu.VMEM((nx, per, chunk, tok), BF16),
             dma((5,)), dma((2, q_width // HEAD_SIZE)), dma((nz, 2)), dma((nz, ny, 2)), dma((n, 2)),
             dma((nz, ny, 2)), dma((nz, ny, 2)), dma((nz, 2)), dma((nz, 2)),
             dma((nx, per)), dma((nx, per)), dma((nx, per)), dma((nx, per)),

time: 46 us -> 46.6 us (1.013)
  the two profiles are of different devices: /device:TPU:20 before, /device:TPU:21 now
where the time goes in v4:
time: 46.6 us; the launch traced here: 46.5 us
  Pallas kernels  44.7 us (96%)
  local copies, waits for them, and re-layouts  1.72 us (4%)
    pallas_call x1, Pallas kernels, shards(): pl.pallas_call(functools.partial(kernel, nz, ny, nx), out_shape=jax.Shape...  44.7 us
    unnamed x1, local copies, waits for them, and re-layouts  1.72 us

profile of v4, /device:TPU:21, one launch (start us, length us, event | category | flops | bytes accessed | tf_op | source)
XLA Modules:
  0.0 46.5 jit_solution(14854470900055292767)
XLA Ops:
  0.0 44.7 %tree_attention_backward.1 = bf16[128,1280]{1,0:T(8,128)(2,1)} custom-call(s32[8,5]{1,0:T(8,128)} %anc_ref.1, bf16[128,1280]{1,0:T(8,128)(2,1)} %q_ref.1, bf16[128,256]{1,0:T(8,128)(2,1)} %k_ref.1, bf16[128,256]{1,0:T(8,128)(2,1)} %v_ref.1, bf16[128,1280]{1,0:T(8,128)(2,1)} %g_ref.1, bf16[5120,1280]{1,0:T(8,128)(2,1)} %wq_ref.1, bf16[5120,256]{1,0:T(8,128)(2,1)} %wk_ref.1, ...), custom_call_target="tpu_custom_call" | custom-call | tf_op jit(solution)/shard_map/tree_attention_backward/pallas_call | solution.py:445
  44.7 1.7 %copy.10 = bf16[128,1280]{1,0:T(8,128)(2,1)} copy(bf16[128,1280]{1,0:T(8,128)(2,1)} %tree_attention_backward.1) | data formatting | bytes 655360

commit v5 on v4

--- a/solution.py
+++ b/solution.py
@@ -89,6 +89,11 @@
     greet(me, x * 2 + 1 - core)
     for dx in range(1, nx):
         greet(me, ((x + dx) % nx) * 2 + core)
+    if deepest < nz * ny:
+        @pl.when(me != deepest)
+        def _():
+            kv_all[deepest] = jnp.zeros_like(kv_all[deepest])
+
     pl.semaphore_wait(barrier, nz - 1 + ny - 1 + 1 + nx - 1)
     for copy in own_kv:
         copy.wait()
@@ -132,6 +137,21 @@
             stats[j, h, 1:2] = jnp.sum(raw, axis=0, keepdims=True)
             stats[j, h, 2:3] = jnp.sum(raw * prob_grads, axis=0, keepdims=True)
 
+    def forward_row(r):
+        pack = pl.ds(r * ny, ny)
+        for h, cols in enumerate(head_cols):
+            keys = kv_all[pack, 0, :, cols].reshape(ny * tok, HEAD_SIZE)
+            values = kv_all[pack, 1, :, cols].reshape(ny * tok, HEAD_SIZE)
+            scores = dot(keys, q_rows[h], BY_LAST).reshape(ny, tok, rows)
+            highest = jnp.max(scores, axis=1, keepdims=True)
+            raw = jnp.exp2((scores - highest) * power)
+            prob_grads = dot(values, g_rows[h], BY_LAST).reshape(ny, tok, rows)
+            s_scr[pack, h] = raw
+            p_scr[pack, h] = prob_grads
+            stats[pack, h, 0:1] = highest
+            stats[pack, h, 1:2] = jnp.sum(raw, axis=1, keepdims=True)
+            stats[pack, h, 2:3] = jnp.sum(raw * prob_grads, axis=1, keepdims=True)
+
     def start_block(r, half, first):
         @pl.when((r * ny + y != deepest) & (z < nz - 1))
         def _():
@@ -153,7 +173,14 @@
             def _():
                 for half in range(2):
                     kv_arrival(r * ny + yy, half)
-                forward(r * ny + yy, False)
+
+                @pl.when(r == z)
+                def _():
+                    forward(r * ny + yy, False)
+
+        @pl.when(r < z)
+        def _():
+            forward_row(r)
 
     for half in range(2):
         start_block(z, half, True)
@@ -182,7 +209,6 @@
             for half in range(2):
                 kv_arrival(r * ny + y, half)
                 start_block(r, half, False)
-            forward(r * ny + y, False)
 
         from_sides(r + 1)
         return carry
@@ -246,6 +272,20 @@
             stage[j, 1, :, cols] = dot(probs.astype(BF16), g_rows[h]).astype(BF16)
             dq_acc[h] += dot(kv_all[j, 0, :, cols].T, score_grads)
 
+    def backward_row(r):
+        pack = pl.ds(r * ny, ny)
+        for h, cols in enumerate(head_cols):
+            probs = s_scr[pack, h] * (stats[pack, h, 0:1] * finals[h, 0:1])
+            score_grads = (probs * (p_scr[pack, h] - finals[h, 1:2])).astype(BF16)
+            score_grads = score_grads.reshape(ny * tok, rows)
+            probs = probs.astype(BF16).reshape(ny * tok, rows)
+            key_grads = (dot(score_grads, q_rows[h]) * factor).astype(BF16)
+            stage[pack, 0, :, cols] = key_grads.reshape(ny, tok, HEAD_SIZE)
+            value_grads = dot(probs, g_rows[h]).astype(BF16)
+            stage[pack, 1, :, cols] = value_grads.reshape(ny, tok, HEAD_SIZE)
+            keys = kv_all[pack, 0, :, cols].reshape(ny * tok, HEAD_SIZE)
+            dq_acc[h] += dot(keys.T, score_grads)
+
     def chain(r):
         j = r * ny + y
         live = j != deepest
@@ -265,18 +305,25 @@
                 z_copy(r, half).start()
 
     def back_step(r, carry):
+        @pl.when(r < z)
+        def _():
+            backward_row(r)
+
         for dy in range(1, ny):
             yy = (y + dy) % ny
 
             @pl.when(y_sends(r, yy))
             def _():
-                backward(r * ny + yy)
+                @pl.when(r == z)
+                def _():
+                    backward(r * ny + yy)
+
                 for half in range(2):
                     y_copy(r, yy, half).start()
 
-        @pl.when((r * ny + y != deepest) | (r == z))
-        def _():
-            backward(r * ny + y)
+        @pl.when(r == z)
+        def _():
+            backward(me)
 
         @pl.when((r > 0) & ((r - 1) * ny + y != deepest))
         def _():

time: 46.6 us -> 47.3 us (1.015)
  the two profiles are of different devices: /device:TPU:21 before, /device:TPU:0 now
where the time goes in v5:
time: 47.3 us; the launch traced here: 47.1 us
  Pallas kernels  45.4 us (96%)
  local copies, waits for them, and re-layouts  1.72 us (4%)
    pallas_call x1, Pallas kernels, shards(): pl.pallas_call(functools.partial(kernel, nz, ny, nx), out_shape=jax.Shape...  45.4 us
    unnamed x1, local copies, waits for them, and re-layouts  1.72 us

profile of v5, /device:TPU:0, one launch (start us, length us, event | category | flops | bytes accessed | tf_op | source)
XLA Modules:
  0.0 47.1 jit_solution(9104736493678103)
XLA Ops:
  0.0 45.4 %tree_attention_backward.1 = bf16[128,1280]{1,0:T(8,128)(2,1)} custom-call(s32[8,5]{1,0:T(8,128)} %anc_ref.1, bf16[128,1280]{1,0:T(8,128)(2,1)} %q_ref.1, bf16[128,256]{1,0:T(8,128)(2,1)} %k_ref.1, bf16[128,256]{1,0:T(8,128)(2,1)} %v_ref.1, bf16[128,1280]{1,0:T(8,128)(2,1)} %g_ref.1, bf16[5120,1280]{1,0:T(8,128)(2,1)} %wq_ref.1, bf16[5120,256]{1,0:T(8,128)(2,1)} %wk_ref.1, ...), custom_call_target="tpu_custom_call" | custom-call | tf_op jit(solution)/shard_map/tree_attention_backward/pallas_call | solution.py:492
  45.4 1.7 %copy.10 = bf16[128,1280]{1,0:T(8,128)(2,1)} copy(bf16[128,1280]{1,0:T(8,128)(2,1)} %tree_attention_backward.1) | data formatting | bytes 655360
